TPU v7x, 512 devices: a whole 4x4x16 slice. The times are simulated.
512 devices in a mesh: face: 4 (over z_lo), tile: 64 (over y, z_hi, x), lev: 2 (over core).
Axes of the slice: x: 4, y: 4, z: 16 (z_hi: 4, z_lo: 4; z = z_hi * 4 + z_lo), core: 2. Of those that a mesh axis runs over, the one named last changes fastest.
Arguments:
- flux: float32 [2048, 8, 512], P(('face', 'tile')), may hold values from -6 to 6
- profile: float32 [16], P('lev'), may hold values from 0.2 to 1
- courant: float32 [2, 16, 512, 2048], P(None, 'lev', 'tile', 'face'), may hold values from 0.05 to 0.45
- winds: int32 [2, 16, 512, 2048], P(None, 'lev', 'tile', 'face'), may hold values from 0 to 1
- cells: int32 [64, 4, 128], P('tile', 'face'), may hold values from 0 to 4095, as said below
- counts: int32 [64, 4], P('tile', 'face'), may hold values from 32 to 128, as said below
- kernels: float32 [16, 64, 4, 128], P('lev', 'tile', 'face'), may hold values from 0.25 to 0.75
- month_weight: float32 [8, 64, 4, 128], P(None, 'tile', 'face'), may hold values from 0 to 1
- observed: float32 [64, 4, 128], P('tile', 'face'), may hold values from -8 to 8
- obs_weight: float32 [64, 4, 128], P('tile', 'face'), may hold values from 0.5 to 2
- precision: float32 [8], replicated, may hold values from 0.5 to 2
Outputs:
- flux_gradient: float32 [8, 512, 2048], P(None, 'tile', 'face')
- precision_gradient: float32 [8], replicated
Inputs may be any that keep to these rules, and one draw needn't show every extreme that they name: Within each block the 128 entries are distinct cells, numbered row by row over the block's 8 rows of 512 cells; the first four slots of every block hold, in some order, a cell of the block's first column, one of its last column, and interior cells of its first row and of its last row. `counts`: slot s of a block holds a sounding when s is below the block's count; some block is full and some holds exactly 32.
All inputs are finite; a program needn't handle non-finite values.
Results may differ from a plain program's by a relative error of at most 0.00015.
Values sent between devices are 32-bit elements; how exact they have to be, the bound alone decides.
A program may use at most 64 MiB of HBM per device.

v0:
```python
import jax
import jax.numpy as jnp
from jax import lax
from jax.sharding import PartitionSpec as P

KAPPA = 0.025


def extended(x, sides, width, wrap):
    for axis, dim in sides:
        devices, length = (lax.axis_size(axis), x.shape[dim])
        up = [(i, (i + 1) % devices) for i in range(devices if wrap else devices - 1)]
        down = [(j, i) for i, j in up]
        last = lax.slice_in_dim(x, length - width, length, axis=dim)
        initial = lax.slice_in_dim(x, 0, width, axis=dim)
        before = lax.ppermute(last, axis, up)
        after = lax.ppermute(initial, axis, down)
        x = jnp.concatenate([before, x, after], axis=dim)
    return x


def shifted(x, axis, by):
    devices = lax.axis_size(axis)
    return lax.ppermute(x, axis, [(i, (i + by) % devices) for i in range(devices)])


def shifted_2(value, axis, steps):
    count = lax.axis_size(axis)
    initial, last = (max(0, -steps), min(count, count - steps))
    return lax.ppermute(value, axis, [(source, source + steps) for source in range(initial, last)])


def weights_from(speed_x, speed_y, east_flag, north_flag):
    w_west = speed_x * (1.0 - east_flag) + KAPPA
    w_east = speed_x * east_flag + KAPPA
    w_south = speed_y * (1.0 - north_flag) + KAPPA
    w_north = speed_y * north_flag + KAPPA
    w_centre = 1.0 - speed_x - speed_y - 4.0 * KAPPA
    return (w_centre, w_west, w_east, w_south, w_north)


def flags_of(winds):
    return ((winds[0] == 1).astype(jnp.float32), (winds[1] == 1).astype(jnp.float32))


def advance(conc, coeffs):
    w_centre, w_west, w_east, w_south, w_north = coeffs
    side = extended(conc, (("face", 3),), 1, True)
    rim = extended(conc, (("tile", 2),), 1, False)
    return (
        w_centre * conc
        + w_west * side[..., :-2]
        + w_east * side[..., 2:]
        + w_south * rim[..., :-2, :]
        + w_north * rim[..., 2:, :]
    )


def retreat(grad, coeffs):
    w_centre, w_west, w_east, w_south, w_north = coeffs
    west_weighted = w_west * grad
    east_weighted = w_east * grad
    south_weighted = w_south * grad
    north_weighted = w_north * grad
    from_east = shifted(west_weighted[..., :1], "face", -1)
    from_west = shifted(east_weighted[..., -1:], "face", 1)
    from_above = shifted_2(south_weighted[..., :1, :], "tile", -1)
    from_below = shifted_2(north_weighted[..., -1:, :], "tile", 1)
    west_part = jnp.concatenate([west_weighted[..., 1:], from_east], -1)
    east_part = jnp.concatenate([from_west, east_weighted[..., :-1]], -1)
    south_part = jnp.concatenate([south_weighted[..., 1:, :], from_above], -2)
    north_part = jnp.concatenate([from_below, north_weighted[..., :-1, :]], -2)
    return w_centre * grad + west_part + east_part + south_part + north_part


def on_device(
    flux,
    profile,
    courant,
    winds,
    cells,
    counts,
    kernels,
    month_weight,
    observed,
    obs_weight,
    precision,
):
    n_tracer = flux.shape[1]
    n_level = profile.shape[0]
    slot_total = cells.shape[2]
    moved = lax.all_to_all(flux, "tile", split_axis=2, concat_axis=0, tiled=True)
    field = jnp.transpose(moved, (1, 2, 0))
    rows_dev = field.shape[1]
    cols_dev = field.shape[2]
    n_cell = rows_dev * cols_dev
    east_flag, north_flag = flags_of(winds)
    conc = profile[None, :, None, None] * field[:, None]
    coeffs = weights_from(courant[0], courant[1], east_flag, north_flag)
    conc = advance(advance(conc, coeffs), coeffs)
    slot_cells = cells.reshape(slot_total)
    live = jnp.arange(slot_total, dtype=jnp.int32) < counts.reshape(())
    picker = jnp.where(
        live[:, None] & (slot_cells[:, None] == jnp.arange(n_cell, dtype=jnp.int32)[None, :]),
        1.0,
        0.0,
    ).astype(jnp.float32)
    flat = conc.reshape(n_tracer, n_level, n_cell)
    sampled = jnp.einsum("tlc,sc->tls", flat, picker, precision=lax.Precision.HIGHEST)
    kern = kernels.reshape(n_level, slot_total)
    monthly = month_weight.reshape(n_tracer, slot_total)
    partial_model = jnp.sum(kern * jnp.sum(monthly[:, None, :] * sampled, 0), 0)
    model = lax.psum(partial_model, "lev")
    forcing = jnp.where(
        live, obs_weight.reshape(slot_total) * (observed.reshape(slot_total) - model), 0.0
    )
    values = kern[None] * (monthly * forcing[None])[:, None, :]
    lam = jnp.einsum("tls,sc->tlc", values, picker, precision=lax.Precision.HIGHEST)
    lam = lam.reshape(n_tracer, n_level, rows_dev, cols_dev)
    lam = retreat(retreat(lam, coeffs), coeffs)
    adj_part = jnp.sum(profile[None, :, None, None] * lam, 1)
    all_cells = n_cell * lax.axis_size("tile") * lax.axis_size("face")
    adj = lax.psum(adj_part, "lev")
    flux_gradient = precision[:, None, None] * field - adj
    square_sum = lax.psum(jnp.sum(adj * adj, axis=(1, 2)), ("face", "tile"))
    precision_gradient = 0.5 / precision - 0.5 * (square_sum / all_cells) / (precision * precision)
    return (flux_gradient, precision_gradient)


def solution(mesh):
    return jax.shard_map(
        on_device,
        mesh=mesh,
        in_specs=(
            P(("face", "tile"), None, None),
            P("lev"),
            P(None, "lev", "tile", "face"),
            P(None, "lev", "tile", "face"),
            P("tile", "face", None),
            P("tile", "face"),
            P("lev", "tile", "face", None),
            P(None, "tile", "face", None),
            P("tile", "face", None),
            P("tile", "face", None),
            P(),
        ),
        out_specs=(P(None, "tile", "face"), P()),
        check_vma=False,
    )
```

profile of v0, /device:TPU:32, one launch (start us, length us, event | category | flops | bytes accessed | tf_op | source)
XLA Modules:
  0.0 1168.7 jit_solution(5610475102505204907)
XLA Ops:
  7.2 1.7 copy.25
  8.9 1.7 reshape.69
  10.6 20.3 %all-to-all-start = ((f32[64,1,512]{2,1,0:T(1,128)}), f32[64,1,512]{2,1,0:T(1,128)S(1)}, u32[]{:S(2)}, u32[]{:S(2)}) async-start(f32[64,1,512]{2,1,0:T(1,128)} %reshape.69), calls=%async_computation | async-start | bytes 262144 | tf_op jit(solution)/shard_map/all_to_all | solution.py:92
  31.1 20.0 %all-to-all-done = f32[64,1,512]{2,1,0:T(1,128)S(1)} async-done(((f32[64,1,512]{2,1,0:T(1,128)}), f32[64,1,512]{2,1,0:T(1,128)S(1)}, u32[]{:S(2)}, u32[]{:S(2)}) %all-to-all-start) | async-done | bytes 131104 | tf_op jit(solution)/shard_map/all_to_all | solution.py:92
  51.1 0.5 broadcast.82
  51.6 0.9 reduce.1
  52.6 1.1 reshape.70
  53.7 2.4 copy.27
  56.1 2.8 all_to_all.16
  59.3 2.5 collective-permute-start.2
  61.8 1.3 collective-permute-start.3
  63.1 2.9 collective-permute-start
  66.1 2.9 collective-permute-start.1
  70.1 4.1 collective-permute-done
  74.2 7.7 collective-permute-done.1
  81.9 0.8 fusion.24
  82.7 1.3 collective-permute-start.6
  84.0 1.3 collective-permute-start.7
  85.5 5.5 collective-permute-start.4
  91.0 1.9 collective-permute-start.5
  93.0 7.6 collective-permute-done.4
  100.5 0.8 fusion.16
  101.3 2.4 fusion.12
  103.8 2.6 psum.21
  106.5 1.7 fusion
  108.2 0.6 broadcast_multiply_fusion.5
  108.8 1.3 collective-permute-start.10
  110.1 4.9 collective-permute-start.11
  115.2 3.2 collective-permute-start.8
  118.4 3.1 collective-permute-start.9
  121.8 0.3 slice.160
  122.2 3.8 collective-permute-done.8
  126.0 6.6 collective-permute-done.9
  132.5 1.1 broadcast_multiply_fusion.6
  133.6 4.2 collective-permute-start.12
  138.1 0.3 slice.168
  138.6 5.9 collective-permute-start.15
  144.5 1.3 collective-permute-start.14
  146.0 3.7 collective-permute-start.13
  149.8 7.5 collective-permute-done.13
  157.3 0.3 pad_maximum_fusion.13
  157.8 9.1 collective-permute-done.14
  167.0 1.1 multiply_reduce_fusion
  168.1 0.7 copy.38
  168.8 66.5 %all-reduce.2.cloned.1.call-done = f32[8,8,512]{2,1,0:T(8,128)} async-done(((f32[8,8,512]{2,1,0:T(8,128)}), f32[8,8,512]{2,1,0:T(8,128)}) %all-reduce.2.cloned.1.call-update) | async-done | bytes 131088 | tf_op jit(solution)/shard_map/psum | solution.py:123
  235.3 1.7 multiply_reduce_fusion.1
  237.0 924.4 %psum.23 = f32[8]{0:T(128)S(1)} all-reduce(f32[8]{0:T(128)S(1)} %get-tuple-element.33), channel_id=1, replica_groups=mesh['face'=4,'tile'=64,'lev'=2] {'face','tile'}, use_global_device_ids=true, to_apply=%region_6.7 | all-reduce | flops 8 | bytes 64 | tf_op jit(solution)/shard_map/psum | solution.py:125
  1161.3 0.5 divide_subtract_fusion
  (62 shorter events, 2.5 us)
Async XLA Ops:
  7.2 23.8 %copy-start = (f32[2,8,8,512]{3,2,1,0:T(8,128)S(1)}, f32[2,8,8,512]{3,2,1,0:T(8,128)}, u32[]{:S(2)}) copy-start(f32[2,8,8,512]{3,2,1,0:T(8,128)} %param.13) | copy-start | bytes 786436
  7.2 23.8 %copy-start.1 = (s32[2,8,8,512]{3,2,1,0:T(8,128)S(1)}, s32[2,8,8,512]{3,2,1,0:T(8,128)}, u32[]{:S(2)}) copy-start(s32[2,8,8,512]{3,2,1,0:T(8,128)} %param.14) | copy-start | bytes 786436
  10.6 40.5 %all-to-all-start = ((f32[64,1,512]{2,1,0:T(1,128)}), f32[64,1,512]{2,1,0:T(1,128)S(1)}, u32[]{:S(2)}, u32[]{:S(2)}) async-start(f32[64,1,512]{2,1,0:T(1,128)} %reshape.69), calls=%async_computation | async-start | bytes 262144 | tf_op jit(solution)/shard_map/all_to_all | solution.py:92
  30.9 204.3 %all-reduce.2.cloned.1.call-start = ((), (), s32[]{:S(2)}) async-start(), calls=%async_computation.1 | async-start | bytes 262144 | tf_op jit(solution)/shard_map/psum | solution.py:123
  56.1 2.8 copy-start.4
  59.3 22.6 %collective-permute-start.2 = (f32[8,8,1,512]{3,1,2,0:T(8,128)S(1)}, f32[8,8,1,512]{3,1,2,0:T(8,128)S(1)}, u32[]{:S(2)}, u32[]{:S(2)}) collective-permute-start(f32[8,8,1,512]{3,1,2,0:T(8,128)S(1)} %get-tuple-element.25), channel_id=1, source_target_pairs={{0,2},{2,4},{4,6},{6,8},{8,10},{10,12},{12,14},{14,16},{16,18},{18... | collective-permute-start | bytes 393224 | tf_op jit(solution)/shard_map/ppermute | solution.py:16
  61.8 20.1 %collective-permute-start.3 = (f32[8,8,1,512]{3,1,2,0:T(8,128)S(1)}, f32[8,8,1,512]{3,1,2,0:T(8,128)S(1)}, u32[]{:S(2)}, u32[]{:S(2)}) collective-permute-start(f32[8,8,1,512]{3,1,2,0:T(8,128)S(1)} %get-tuple-element.26), channel_id=1, source_target_pairs={{2,0},{4,2},{6,4},{8,6},{10,8},{12,10},{14,12},{16,14},{18,16},{20... | collective-permute-start | bytes 393224 | tf_op jit(solution)/shard_map/ppermute | solution.py:17
  63.1 11.1 collective-permute-start
  66.1 15.9 %collective-permute-start.1 = (f32[8,8,8,1]{3,1,2,0:T(8,128)S(1)}, f32[8,8,8,1]{3,1,2,0:T(8,128)S(1)}, u32[]{:S(2)}, u32[]{:S(2)}) collective-permute-start(f32[8,8,8,1]{3,1,2,0:T(8,128)S(1)} %get-tuple-element.24), channel_id=1, source_target_pairs={{128,0},{256,128},{384,256},{0,384},{129,1},{257,129},{385,257},{1... | collective-permute-start | bytes 6152 | tf_op jit(solution)/shard_map/ppermute | solution.py:17
  82.7 17.8 %collective-permute-start.6 = (f32[8,8,1,512]{3,1,2,0:T(8,128)S(1)}, f32[8,8,1,512]{3,1,2,0:T(8,128)S(1)}, u32[]{:S(2)}, u32[]{:S(2)}) collective-permute-start(f32[8,8,1,512]{3,1,2,0:T(8,128)S(1)} %get-tuple-element.21), channel_id=1, source_target_pairs={{0,2},{2,4},{4,6},{6,8},{8,10},{10,12},{12,14},{14,16},{16,18},{18... | collective-permute-start | bytes 393224 | tf_op jit(solution)/shard_map/ppermute | solution.py:16
  84.0 17.3 %copy-start.2 = (f32[8,1,1,128]{3,2,1,0:T(1,128)S(1)}, f32[8,1,1,128]{3,2,1,0:T(1,128)}, u32[]{:S(2)}) copy-start(f32[8,1,1,128]{3,2,1,0:T(1,128)} %param.18) | copy-start | bytes 12292
  84.0 17.3 %copy-start.8 = (s32[1,1,128]{2,1,0:T(1,128)S(1)}, s32[1,1,128]{2,1,0:T(1,128)}, u32[]{:S(2)}) copy-start(s32[1,1,128]{2,1,0:T(1,128)} %param.15) | copy-start | bytes 1540
  84.0 16.5 %collective-permute-start.7 = (f32[8,8,1,512]{3,1,2,0:T(8,128)S(1)}, f32[8,8,1,512]{3,1,2,0:T(8,128)S(1)}, u32[]{:S(2)}, u32[]{:S(2)}) collective-permute-start(f32[8,8,1,512]{3,1,2,0:T(8,128)S(1)} %get-tuple-element.22), channel_id=1, source_target_pairs={{2,0},{4,2},{6,4},{8,6},{10,8},{12,10},{14,12},{16,14},{18,16},{20... | collective-permute-start | bytes 393224 | tf_op jit(solution)/shard_map/ppermute | solution.py:17
  85.5 15.0 %collective-permute-start.4 = (f32[8,8,8,1]{3,1,2,0:T(8,128)S(1)}, f32[8,8,8,1]{3,1,2,0:T(8,128)S(1)}, u32[]{:S(2)}, u32[]{:S(2)}) collective-permute-start(f32[8,8,8,1]{3,1,2,0:T(8,128)S(1)} %get-tuple-element.19), channel_id=1, source_target_pairs={{0,128},{128,256},{256,384},{384,0},{1,129},{129,257},{257,385},{3... | collective-permute-start | bytes 6152 | tf_op jit(solution)/shard_map/ppermute | solution.py:16
  91.0 9.6 collective-permute-start.5
  92.9 10.9 copy-start.3
  92.9 13.5 %copy-start.6 = (f32[1,1,128]{2,1,0:T(1,128)S(1)}, f32[1,1,128]{2,1,0:T(1,128)}, u32[]{:S(2)}) copy-start(f32[1,1,128]{2,1,0:T(1,128)} %param.19) | copy-start | bytes 1540
  92.9 13.5 %copy-start.7 = (f32[1,1,128]{2,1,0:T(1,128)S(1)}, f32[1,1,128]{2,1,0:T(1,128)}, u32[]{:S(2)}) copy-start(f32[1,1,128]{2,1,0:T(1,128)} %param.20) | copy-start | bytes 1540
  108.8 23.7 %collective-permute-start.10 = (f32[8,8,1,512]{3,1,2,0:T(8,128)S(1)}, f32[8,8,1,512]{3,1,2,0:T(8,128)S(1)}, u32[]{:S(2)}, u32[]{:S(2)}) collective-permute-start(f32[8,8,1,512]{3,1,2,0:T(8,128)S(1)} %slice.165), channel_id=1, source_target_pairs={{2,0},{4,2},{6,4},{8,6},{10,8},{12,10},{14,12},{16,14},{18,16},{20... | collective-permute-start | bytes 393224 | tf_op jit(solution)/shard_map/ppermute | solution.py:30
  110.1 22.4 %collective-permute-start.11 = (f32[8,8,1,512]{3,1,2,0:T(8,128)S(1)}, f32[8,8,1,512]{3,1,2,0:T(8,128)S(1)}, u32[]{:S(2)}, u32[]{:S(2)}) collective-permute-start(f32[8,8,1,512]{3,1,2,0:T(8,128)S(1)} %slice.166), channel_id=1, source_target_pairs={{0,2},{2,4},{4,6},{6,8},{8,10},{10,12},{12,14},{14,16},{16,18},{18... | collective-permute-start | bytes 393224 | tf_op jit(solution)/shard_map/ppermute | solution.py:30
  115.2 10.7 collective-permute-start.8
  118.4 14.1 %collective-permute-start.9 = (f32[8,8,8,1]{3,1,2,0:T(8,128)S(1)}, f32[8,8,8,1]{3,1,2,0:T(8,128)S(1)}, u32[]{:S(2)}, u32[]{:S(2)}) collective-permute-start(f32[8,8,8,1]{3,1,2,0:T(8,128)S(1)} %slice.162), channel_id=1, source_target_pairs={{0,128},{128,256},{256,384},{384,0},{1,129},{129,257},{257,385},{3... | collective-permute-start | bytes 6152 | tf_op jit(solution)/shard_map/ppermute | solution.py:24
  133.6 16.0 %collective-permute-start.12 = (f32[8,8,8,1]{3,1,2,0:T(8,128)S(1)}, f32[8,8,8,1]{3,1,2,0:T(8,128)S(1)}, u32[]{:S(2)}, u32[]{:S(2)}) collective-permute-start(f32[8,8,8,1]{3,1,2,0:T(8,128)S(1)} %slice.169), channel_id=1, source_target_pairs={{0,384},{128,0},{256,128},{384,256},{1,385},{129,1},{257,129},{385... | collective-permute-start | bytes 6152 | tf_op jit(solution)/shard_map/ppermute | solution.py:24
  138.6 19.1 %collective-permute-start.15 = (f32[8,8,1,512]{3,1,2,0:T(8,128)S(1)}, f32[8,8,1,512]{3,1,2,0:T(8,128)S(1)}, u32[]{:S(2)}, u32[]{:S(2)}) collective-permute-start(f32[8,8,1,512]{3,1,2,0:T(8,128)S(1)} %slice.174), channel_id=1, source_target_pairs={{0,2},{2,4},{4,6},{6,8},{8,10},{10,12},{12,14},{14,16},{16,18},{18... | collective-permute-start | bytes 393224 | tf_op jit(solution)/shard_map/ppermute | solution.py:30
  144.5 22.3 %collective-permute-start.14 = (f32[8,8,1,512]{3,1,2,0:T(8,128)S(1)}, f32[8,8,1,512]{3,1,2,0:T(8,128)S(1)}, u32[]{:S(2)}, u32[]{:S(2)}) collective-permute-start(f32[8,8,1,512]{3,1,2,0:T(8,128)S(1)} %slice.173), channel_id=1, source_target_pairs={{2,0},{4,2},{6,4},{8,6},{10,8},{12,10},{14,12},{16,14},{18,16},{20... | collective-permute-start | bytes 393224 | tf_op jit(solution)/shard_map/ppermute | solution.py:30
  146.0 11.4 collective-permute-start.13
  166.9 68.3 %copy-start.5 = (f32[8]{0:T(128)S(1)}, f32[8]{0:T(128)}, u32[]{:S(2)}) copy-start(f32[8]{0:T(128)} %param.21) | copy-start | bytes 100
Sparse Core Ops, SparseCore 0:
  169.0 66.2 all-reduce.1
where the time goes:
time: 1170 us
  blocking collectives  927 us (79%)
  waiting for transfers between devices  133 us (11%)
  starting transfers between devices  67.6 us (6%)
  between operations  15.2 us (1%)
  local copies, waits for them, and re-layouts  13.2 us (1%)
    psum x1, blocking collectives, on_device(): square_sum = lax.psum(jnp.sum(adj * adj, axis=(1, 2)), ('face', 'tile'))  924 us
    psum x1, waiting for transfers between devices, on_device(): adj = lax.psum(adj_part, 'lev')  66.5 us
  transfers between devices with their start and end apart: 18, of which 9 were waited for; matrix products, arithmetic and copies ran while one was open for 0% of the time, Pallas kernels for 0%

commit v1 on v0

--- a/solution.py
+++ b/solution.py
@@ -122,7 +122,7 @@
     all_cells = n_cell * lax.axis_size("tile") * lax.axis_size("face")
     adj = lax.psum(adj_part, "lev")
     flux_gradient = precision[:, None, None] * field - adj
-    square_sum = lax.psum(jnp.sum(adj * adj, axis=(1, 2)), ("face", "tile"))
+    square_sum = lax.psum(lax.psum(jnp.sum(adj * adj, axis=(1, 2)), "tile"), "face")
     precision_gradient = 0.5 / precision - 0.5 * (square_sum / all_cells) / (precision * precision)
     return (flux_gradient, precision_gradient)
 

time: 1170 us -> 480 us (0.41)
  blocking collectives: 927 us -> 237 us
    psum x1 -> x2, blocking collectives: 924 us -> 235 us  [the longest x1 225 us: on_device(): lax.psum(jnp.sum(adj * adj, axis=(1, 2)), 'tile')]
  transfers between devices with their start and end apart: 18 -> 18, of which waited for: 9 -> 9; matrix products, arithmetic and copies ran while one was open for 0% -> 1% of each run, Pallas kernels for 0% -> 0%
where the time goes in v1:
time: 480 us; the launch traced here: 479 us
  blocking collectives  237 us (49%)
  waiting for transfers between devices  133 us (28%)
  starting transfers between devices  67.6 us (14%)
  between operations  15.2 us (3%)
  local copies, waits for them, and re-layouts  13.2 us (3%)
  other arithmetic  8.64 us (2%)
    psum x1, blocking collectives, on_device(): lax.psum(jnp.sum(adj * adj, axis=(1, 2)), 'tile')  225 us
    psum x1, waiting for transfers between devices, on_device(): adj = lax.psum(adj_part, 'lev')  66.4 us
    all_to_all x1, starting transfers between devices, on_device(): lax.all_to_all(flux, 'tile', split_axis=2, concat_axis=0, tiled=True)  20.3 us
    all_to_all x1, waiting for transfers between devices, on_device(): lax.all_to_all(flux, 'tile', split_axis=2, concat_axis=0, tiled=True)  20 us
    ppermute x4, waiting for transfers between devices, shifted(): lax.ppermute(x, axis, [(i, (i + by) % devices) for i in range(devices)])  17.9 us
    ppermute x4, starting transfers between devices, shifted(): lax.ppermute(x, axis, [(i, (i + by) % devices) for i in range(devices)])  14.3 us
    ppermute x4, starting transfers between devices, shifted_2(): lax.ppermute(value, axis, [(source, source + steps) for source in range(i...  13.4 us
    ppermute x4, starting transfers between devices, extended(): before = lax.ppermute(last, axis, up)  12.2 us
  transfers between devices with their start and end apart: 18, of which 9 were waited for; matrix products, arithmetic and copies ran while one was open for 1% of the time, Pallas kernels for 0%

profile of v1, /device:TPU:32, one launch (start us, length us, event | category | flops | bytes accessed | tf_op | source)
XLA Modules:
  0.0 479.2 jit_solution(5228826029167741256)
XLA Ops:
  7.2 1.7 copy.25
  8.9 1.7 reshape.69
  10.6 20.3 %all-to-all-start = ((f32[64,1,512]{2,1,0:T(1,128)}), f32[64,1,512]{2,1,0:T(1,128)S(1)}, u32[]{:S(2)}, u32[]{:S(2)}) async-start(f32[64,1,512]{2,1,0:T(1,128)} %reshape.69), calls=%async_computation | async-start | bytes 262144 | tf_op jit(solution)/shard_map/all_to_all | solution.py:92
  31.1 20.0 %all-to-all-done = f32[64,1,512]{2,1,0:T(1,128)S(1)} async-done(((f32[64,1,512]{2,1,0:T(1,128)}), f32[64,1,512]{2,1,0:T(1,128)S(1)}, u32[]{:S(2)}, u32[]{:S(2)}) %all-to-all-start) | async-done | bytes 131104 | tf_op jit(solution)/shard_map/all_to_all | solution.py:92
  51.1 0.5 broadcast.82
  51.6 0.9 reduce.1
  52.6 1.1 reshape.70
  53.7 2.4 copy.27
  56.1 2.8 all_to_all.16
  59.3 2.5 collective-permute-start.2
  61.8 1.3 collective-permute-start.3
  63.1 2.9 collective-permute-start
  66.1 2.9 collective-permute-start.1
  70.1 4.1 collective-permute-done
  74.2 7.7 %collective-permute-done.1 = f32[8,8,8,1]{3,1,2,0:T(8,128)S(1)} collective-permute-done((f32[8,8,8,1]{3,1,2,0:T(8,128)S(1)}, f32[8,8,8,1]{3,1,2,0:T(8,128)S(1)}, u32[]{:S(2)}, u32[]{:S(2)}) %collective-permute-start.1) | collective-permute-done | bytes 2080 | tf_op jit(solution)/shard_map/ppermute | solution.py:17
  81.9 0.8 fusion.24
  82.7 1.3 collective-permute-start.6
  84.0 1.3 collective-permute-start.7
  85.5 5.5 %collective-permute-start.4 = (f32[8,8,8,1]{3,1,2,0:T(8,128)S(1)}, f32[8,8,8,1]{3,1,2,0:T(8,128)S(1)}, u32[]{:S(2)}, u32[]{:S(2)}) collective-permute-start(f32[8,8,8,1]{3,1,2,0:T(8,128)S(1)} %get-tuple-element.19), channel_id=1, source_target_pairs={{0,128},{128,256},{256,384},{384,0},{1,129},{129,257},{257,385},{3... | collective-permute-start | bytes 6152 | tf_op jit(solution)/shard_map/ppermute | solution.py:16
  91.0 1.9 collective-permute-start.5
  93.0 7.6 %collective-permute-done.4 = f32[8,8,8,1]{3,1,2,0:T(8,128)S(1)} collective-permute-done((f32[8,8,8,1]{3,1,2,0:T(8,128)S(1)}, f32[8,8,8,1]{3,1,2,0:T(8,128)S(1)}, u32[]{:S(2)}, u32[]{:S(2)}) %collective-permute-start.4) | collective-permute-done | bytes 2080 | tf_op jit(solution)/shard_map/ppermute | solution.py:16
  100.5 0.8 fusion.16
  101.3 2.5 fusion.12
  103.8 2.6 psum.28
  106.5 1.7 fusion
  108.2 0.6 broadcast_multiply_fusion.5
  108.8 1.3 collective-permute-start.10
  110.1 4.9 %collective-permute-start.11 = (f32[8,8,1,512]{3,1,2,0:T(8,128)S(1)}, f32[8,8,1,512]{3,1,2,0:T(8,128)S(1)}, u32[]{:S(2)}, u32[]{:S(2)}) collective-permute-start(f32[8,8,1,512]{3,1,2,0:T(8,128)S(1)} %slice.166), channel_id=1, source_target_pairs={{0,2},{2,4},{4,6},{6,8},{8,10},{10,12},{12,14},{14,16},{16,18},{18... | collective-permute-start | bytes 393224 | tf_op jit(solution)/shard_map/ppermute | solution.py:30
  115.2 3.2 collective-permute-start.8
  118.4 3.1 collective-permute-start.9
  121.8 0.3 slice.160
  122.2 3.8 collective-permute-done.8
  126.0 6.6 %collective-permute-done.9 = f32[8,8,8,1]{3,1,2,0:T(8,128)S(1)} collective-permute-done((f32[8,8,8,1]{3,1,2,0:T(8,128)S(1)}, f32[8,8,8,1]{3,1,2,0:T(8,128)S(1)}, u32[]{:S(2)}, u32[]{:S(2)}) %collective-permute-start.9) | collective-permute-done | bytes 2080 | tf_op jit(solution)/shard_map/ppermute | solution.py:24
  132.5 1.1 broadcast_multiply_fusion.6
  133.6 4.2 collective-permute-start.12
  138.6 5.9 %collective-permute-start.15 = (f32[8,8,1,512]{3,1,2,0:T(8,128)S(1)}, f32[8,8,1,512]{3,1,2,0:T(8,128)S(1)}, u32[]{:S(2)}, u32[]{:S(2)}) collective-permute-start(f32[8,8,1,512]{3,1,2,0:T(8,128)S(1)} %slice.174), channel_id=1, source_target_pairs={{0,2},{2,4},{4,6},{6,8},{8,10},{10,12},{12,14},{14,16},{16,18},{18... | collective-permute-start | bytes 393224 | tf_op jit(solution)/shard_map/ppermute | solution.py:30
  144.5 1.3 collective-permute-start.14
  146.0 3.7 collective-permute-start.13
  149.8 7.5 %collective-permute-done.13 = f32[8,8,8,1]{3,1,2,0:T(8,128)S(1)} collective-permute-done((f32[8,8,8,1]{3,1,2,0:T(8,128)S(1)}, f32[8,8,8,1]{3,1,2,0:T(8,128)S(1)}, u32[]{:S(2)}, u32[]{:S(2)}) %collective-permute-start.13) | collective-permute-done | bytes 2080 | tf_op jit(solution)/shard_map/ppermute | solution.py:24
  157.3 0.3 pad_maximum_fusion.13
  157.8 9.1 %collective-permute-done.14 = f32[8,8,1,512]{3,1,2,0:T(8,128)S(1)} collective-permute-done((f32[8,8,1,512]{3,1,2,0:T(8,128)S(1)}, f32[8,8,1,512]{3,1,2,0:T(8,128)S(1)}, u32[]{:S(2)}, u32[]{:S(2)}) %collective-permute-start.14) | collective-permute-done | bytes 131104 | tf_op jit(solution)/shard_map/ppermute | solution.py:30
  167.0 1.1 multiply_reduce_fusion
  168.1 0.7 copy.38
  168.8 66.4 %all-reduce.2.cloned.1.call-done = f32[8,8,512]{2,1,0:T(8,128)} async-done(((f32[8,8,512]{2,1,0:T(8,128)}), f32[8,8,512]{2,1,0:T(8,128)}) %all-reduce.2.cloned.1.call-update) | async-done | bytes 131088 | tf_op jit(solution)/shard_map/psum | solution.py:123
  235.3 1.7 multiply_reduce_fusion.1
  237.0 224.8 %psum.30 = f32[8]{0:T(128)S(1)} all-reduce(f32[8]{0:T(128)S(1)} %get-tuple-element.33), channel_id=1, replica_groups=mesh['face'=4,'tile'=64,'lev'=2] {'tile'}, use_global_device_ids=true, to_apply=%region_6.7 | all-reduce | flops 8 | bytes 64 | tf_op jit(solution)/shard_map/psum | solution.py:125
  461.8 10.0 %psum.31 = f32[8]{0:T(128)S(1)} all-reduce(f32[8]{0:T(128)S(1)} %psum.30), channel_id=1, replica_groups=mesh['face'=4,'tile'=64,'lev'=2] {'face'}, use_global_device_ids=true, to_apply=%region_7.8 | all-reduce | flops 8 | bytes 64 | tf_op jit(solution)/shard_map/psum | solution.py:125
  471.8 0.5 divide_subtract_fusion
  (63 shorter events, 2.8 us)
Async XLA Ops:
  7.2 23.8 %copy-start = (f32[2,8,8,512]{3,2,1,0:T(8,128)S(1)}, f32[2,8,8,512]{3,2,1,0:T(8,128)}, u32[]{:S(2)}) copy-start(f32[2,8,8,512]{3,2,1,0:T(8,128)} %param.13) | copy-start | bytes 786436
  7.2 23.8 %copy-start.1 = (s32[2,8,8,512]{3,2,1,0:T(8,128)S(1)}, s32[2,8,8,512]{3,2,1,0:T(8,128)}, u32[]{:S(2)}) copy-start(s32[2,8,8,512]{3,2,1,0:T(8,128)} %param.14) | copy-start | bytes 786436
  10.6 40.5 %all-to-all-start = ((f32[64,1,512]{2,1,0:T(1,128)}), f32[64,1,512]{2,1,0:T(1,128)S(1)}, u32[]{:S(2)}, u32[]{:S(2)}) async-start(f32[64,1,512]{2,1,0:T(1,128)} %reshape.69), calls=%async_computation | async-start | bytes 262144 | tf_op jit(solution)/shard_map/all_to_all | solution.py:92
  30.9 204.3 %all-reduce.2.cloned.1.call-start = ((), (), s32[]{:S(2)}) async-start(), calls=%async_computation.1 | async-start | bytes 262144 | tf_op jit(solution)/shard_map/psum | solution.py:123
  56.1 2.8 copy-start.4
  59.3 22.6 %collective-permute-start.2 = (f32[8,8,1,512]{3,1,2,0:T(8,128)S(1)}, f32[8,8,1,512]{3,1,2,0:T(8,128)S(1)}, u32[]{:S(2)}, u32[]{:S(2)}) collective-permute-start(f32[8,8,1,512]{3,1,2,0:T(8,128)S(1)} %get-tuple-element.25), channel_id=1, source_target_pairs={{0,2},{2,4},{4,6},{6,8},{8,10},{10,12},{12,14},{14,16},{16,18},{18... | collective-permute-start | bytes 393224 | tf_op jit(solution)/shard_map/ppermute | solution.py:16
  61.8 20.1 %collective-permute-start.3 = (f32[8,8,1,512]{3,1,2,0:T(8,128)S(1)}, f32[8,8,1,512]{3,1,2,0:T(8,128)S(1)}, u32[]{:S(2)}, u32[]{:S(2)}) collective-permute-start(f32[8,8,1,512]{3,1,2,0:T(8,128)S(1)} %get-tuple-element.26), channel_id=1, source_target_pairs={{2,0},{4,2},{6,4},{8,6},{10,8},{12,10},{14,12},{16,14},{18,16},{20... | collective-permute-start | bytes 393224 | tf_op jit(solution)/shard_map/ppermute | solution.py:17
  63.1 11.1 %collective-permute-start = (f32[8,8,8,1]{3,1,2,0:T(8,128)S(1)}, f32[8,8,8,1]{3,1,2,0:T(8,128)S(1)}, u32[]{:S(2)}, u32[]{:S(2)}) collective-permute-start(f32[8,8,8,1]{3,1,2,0:T(8,128)S(1)} %get-tuple-element.23), channel_id=1, source_target_pairs={{0,128},{128,256},{256,384},{384,0},{1,129},{129,257},{257,385},{3... | collective-permute-start | bytes 6152 | tf_op jit(solution)/shard_map/ppermute | solution.py:16
  66.1 15.9 %collective-permute-start.1 = (f32[8,8,8,1]{3,1,2,0:T(8,128)S(1)}, f32[8,8,8,1]{3,1,2,0:T(8,128)S(1)}, u32[]{:S(2)}, u32[]{:S(2)}) collective-permute-start(f32[8,8,8,1]{3,1,2,0:T(8,128)S(1)} %get-tuple-element.24), channel_id=1, source_target_pairs={{128,0},{256,128},{384,256},{0,384},{129,1},{257,129},{385,257},{1... | collective-permute-start | bytes 6152 | tf_op jit(solution)/shard_map/ppermute | solution.py:17
  82.7 17.8 %collective-permute-start.6 = (f32[8,8,1,512]{3,1,2,0:T(8,128)S(1)}, f32[8,8,1,512]{3,1,2,0:T(8,128)S(1)}, u32[]{:S(2)}, u32[]{:S(2)}) collective-permute-start(f32[8,8,1,512]{3,1,2,0:T(8,128)S(1)} %get-tuple-element.21), channel_id=1, source_target_pairs={{0,2},{2,4},{4,6},{6,8},{8,10},{10,12},{12,14},{14,16},{16,18},{18... | collective-permute-start | bytes 393224 | tf_op jit(solution)/shard_map/ppermute | solution.py:16
  84.0 17.3 %copy-start.2 = (f32[8,1,1,128]{3,2,1,0:T(1,128)S(1)}, f32[8,1,1,128]{3,2,1,0:T(1,128)}, u32[]{:S(2)}) copy-start(f32[8,1,1,128]{3,2,1,0:T(1,128)} %param.18) | copy-start | bytes 12292
  84.0 17.3 %copy-start.8 = (s32[1,1,128]{2,1,0:T(1,128)S(1)}, s32[1,1,128]{2,1,0:T(1,128)}, u32[]{:S(2)}) copy-start(s32[1,1,128]{2,1,0:T(1,128)} %param.15) | copy-start | bytes 1540
  84.0 16.5 %collective-permute-start.7 = (f32[8,8,1,512]{3,1,2,0:T(8,128)S(1)}, f32[8,8,1,512]{3,1,2,0:T(8,128)S(1)}, u32[]{:S(2)}, u32[]{:S(2)}) collective-permute-start(f32[8,8,1,512]{3,1,2,0:T(8,128)S(1)} %get-tuple-element.22), channel_id=1, source_target_pairs={{2,0},{4,2},{6,4},{8,6},{10,8},{12,10},{14,12},{16,14},{18,16},{20... | collective-permute-start | bytes 393224 | tf_op jit(solution)/shard_map/ppermute | solution.py:17
  85.5 15.0 %collective-permute-start.4 = (f32[8,8,8,1]{3,1,2,0:T(8,128)S(1)}, f32[8,8,8,1]{3,1,2,0:T(8,128)S(1)}, u32[]{:S(2)}, u32[]{:S(2)}) collective-permute-start(f32[8,8,8,1]{3,1,2,0:T(8,128)S(1)} %get-tuple-element.19), channel_id=1, source_target_pairs={{0,128},{128,256},{256,384},{384,0},{1,129},{129,257},{257,385},{3... | collective-permute-start | bytes 6152 | tf_op jit(solution)/shard_map/ppermute | solution.py:16
  91.0 9.6 %collective-permute-start.5 = (f32[8,8,8,1]{3,1,2,0:T(8,128)S(1)}, f32[8,8,8,1]{3,1,2,0:T(8,128)S(1)}, u32[]{:S(2)}, u32[]{:S(2)}) collective-permute-start(f32[8,8,8,1]{3,1,2,0:T(8,128)S(1)} %get-tuple-element.20), channel_id=1, source_target_pairs={{128,0},{256,128},{384,256},{0,384},{129,1},{257,129},{385,257},{1... | collective-permute-start | bytes 6152 | tf_op jit(solution)/shard_map/ppermute | solution.py:17
  92.9 10.9 %copy-start.3 = (f32[8,1,1,128]{3,2,1,0:T(1,128)S(1)}, f32[8,1,1,128]{3,2,1,0:T(1,128)}, u32[]{:S(2)}) copy-start(f32[8,1,1,128]{3,2,1,0:T(1,128)} %param.17) | copy-start | bytes 12292
  92.9 13.5 %copy-start.6 = (f32[1,1,128]{2,1,0:T(1,128)S(1)}, f32[1,1,128]{2,1,0:T(1,128)}, u32[]{:S(2)}) copy-start(f32[1,1,128]{2,1,0:T(1,128)} %param.19) | copy-start | bytes 1540
  92.9 13.5 %copy-start.7 = (f32[1,1,128]{2,1,0:T(1,128)S(1)}, f32[1,1,128]{2,1,0:T(1,128)}, u32[]{:S(2)}) copy-start(f32[1,1,128]{2,1,0:T(1,128)} %param.20) | copy-start | bytes 1540
  108.8 23.7 %collective-permute-start.10 = (f32[8,8,1,512]{3,1,2,0:T(8,128)S(1)}, f32[8,8,1,512]{3,1,2,0:T(8,128)S(1)}, u32[]{:S(2)}, u32[]{:S(2)}) collective-permute-start(f32[8,8,1,512]{3,1,2,0:T(8,128)S(1)} %slice.165), channel_id=1, source_target_pairs={{2,0},{4,2},{6,4},{8,6},{10,8},{12,10},{14,12},{16,14},{18,16},{20... | collective-permute-start | bytes 393224 | tf_op jit(solution)/shard_map/ppermute | solution.py:30
  110.1 22.4 %collective-permute-start.11 = (f32[8,8,1,512]{3,1,2,0:T(8,128)S(1)}, f32[8,8,1,512]{3,1,2,0:T(8,128)S(1)}, u32[]{:S(2)}, u32[]{:S(2)}) collective-permute-start(f32[8,8,1,512]{3,1,2,0:T(8,128)S(1)} %slice.166), channel_id=1, source_target_pairs={{0,2},{2,4},{4,6},{6,8},{8,10},{10,12},{12,14},{14,16},{16,18},{18... | collective-permute-start | bytes 393224 | tf_op jit(solution)/shard_map/ppermute | solution.py:30
  115.2 10.7 %collective-permute-start.8 = (f32[8,8,8,1]{3,1,2,0:T(8,128)S(1)}, f32[8,8,8,1]{3,1,2,0:T(8,128)S(1)}, u32[]{:S(2)}, u32[]{:S(2)}) collective-permute-start(f32[8,8,8,1]{3,1,2,0:T(8,128)S(1)} %slice.161), channel_id=1, source_target_pairs={{0,384},{128,0},{256,128},{384,256},{1,385},{129,1},{257,129},{385... | collective-permute-start | bytes 6152 | tf_op jit(solution)/shard_map/ppermute | solution.py:24
  118.4 14.1 %collective-permute-start.9 = (f32[8,8,8,1]{3,1,2,0:T(8,128)S(1)}, f32[8,8,8,1]{3,1,2,0:T(8,128)S(1)}, u32[]{:S(2)}, u32[]{:S(2)}) collective-permute-start(f32[8,8,8,1]{3,1,2,0:T(8,128)S(1)} %slice.162), channel_id=1, source_target_pairs={{0,128},{128,256},{256,384},{384,0},{1,129},{129,257},{257,385},{3... | collective-permute-start | bytes 6152 | tf_op jit(solution)/shard_map/ppermute | solution.py:24
  133.6 16.0 %collective-permute-start.12 = (f32[8,8,8,1]{3,1,2,0:T(8,128)S(1)}, f32[8,8,8,1]{3,1,2,0:T(8,128)S(1)}, u32[]{:S(2)}, u32[]{:S(2)}) collective-permute-start(f32[8,8,8,1]{3,1,2,0:T(8,128)S(1)} %slice.169), channel_id=1, source_target_pairs={{0,384},{128,0},{256,128},{384,256},{1,385},{129,1},{257,129},{385... | collective-permute-start | bytes 6152 | tf_op jit(solution)/shard_map/ppermute | solution.py:24
  138.6 19.1 %collective-permute-start.15 = (f32[8,8,1,512]{3,1,2,0:T(8,128)S(1)}, f32[8,8,1,512]{3,1,2,0:T(8,128)S(1)}, u32[]{:S(2)}, u32[]{:S(2)}) collective-permute-start(f32[8,8,1,512]{3,1,2,0:T(8,128)S(1)} %slice.174), channel_id=1, source_target_pairs={{0,2},{2,4},{4,6},{6,8},{8,10},{10,12},{12,14},{14,16},{16,18},{18... | collective-permute-start | bytes 393224 | tf_op jit(solution)/shard_map/ppermute | solution.py:30
  144.5 22.3 %collective-permute-start.14 = (f32[8,8,1,512]{3,1,2,0:T(8,128)S(1)}, f32[8,8,1,512]{3,1,2,0:T(8,128)S(1)}, u32[]{:S(2)}, u32[]{:S(2)}) collective-permute-start(f32[8,8,1,512]{3,1,2,0:T(8,128)S(1)} %slice.173), channel_id=1, source_target_pairs={{2,0},{4,2},{6,4},{8,6},{10,8},{12,10},{14,12},{16,14},{18,16},{20... | collective-permute-start | bytes 393224 | tf_op jit(solution)/shard_map/ppermute | solution.py:30
  146.0 11.4 %collective-permute-start.13 = (f32[8,8,8,1]{3,1,2,0:T(8,128)S(1)}, f32[8,8,8,1]{3,1,2,0:T(8,128)S(1)}, u32[]{:S(2)}, u32[]{:S(2)}) collective-permute-start(f32[8,8,8,1]{3,1,2,0:T(8,128)S(1)} %slice.170), channel_id=1, source_target_pairs={{0,128},{128,256},{256,384},{384,0},{1,129},{129,257},{257,385},{3... | collective-permute-start | bytes 6152 | tf_op jit(solution)/shard_map/ppermute | solution.py:24
  166.9 68.3 %copy-start.5 = (f32[8]{0:T(128)S(1)}, f32[8]{0:T(128)}, u32[]{:S(2)}) copy-start(f32[8]{0:T(128)} %param.21) | copy-start | bytes 100
Sparse Core Ops, SparseCore 0:
  169.0 66.2 all-reduce.1
